TPU v7x, 256 devices: a whole 4x4x8 slice. The times are simulated.
256 devices in a mesh: dom: 16 (over x_hi, y, core), shard: 8 (over z), dp: 2 (over x_lo).
Axes of the slice: x: 4 (x_hi: 2, x_lo: 2; x = x_hi * 2 + x_lo), y: 4, z: 8, core: 2. Of those that a mesh axis runs over, the one named last changes fastest.
Arguments:
- queries_in: bfloat16 [16, 2048, 1024], P('dom', ('shard', 'dp')), may hold values from -8 to 8
- encoder_weight: bfloat16 [1024, 1024], P(('dom', 'shard', 'dp')), may hold values from -0.1875 to 0.1875
- codebook: float32 [16, 128, 8, 256], P('dom', 'shard'), may hold values from -0.06 to 0.06
- codes: int32 [16, 8192, 128], P('dom', 'shard'), may hold values from 0 to 255
- positive_ids: int32 [16, 2048], P('dom'), may hold values from 0 to 8191
- loss_weight: bfloat16 [16, 2048], P('dom'), may hold values from 0.5 to 2
Outputs:
- encoder_grad: float32 [1024, 1024], P(('dom', 'shard', 'dp'))
- codebook_grad: float32 [16, 128, 8, 256], P('dom', ('shard', 'dp'))
All inputs are finite; a program needn't handle non-finite values.
Results may differ from a plain program's by a relative error of at most 0.0005.
The roundings to bfloat16 on the way count: a program that leaves them out, or rounds other values in their place, can miss the bound.
Values may be sent and summed in bfloat16 or wider, within the bound.
A program may use at most 64 MiB of HBM per device.

v0:
```python
import functools

import jax
import jax.numpy as jnp
from jax import lax
from jax.experimental import pallas as pl
from jax.experimental.pallas import tpu as pltpu
from jax.sharding import PartitionSpec as P

MESH = pl.DeviceIdType.MESH
BF16 = jnp.bfloat16
F32 = jnp.float32
EPS = 1e-06
NT = (((1,), (1,)), ((), ()))


class Ring:
    def __init__(self, slot, half, me, n, dev, send_sem, recv_sem):
        self.slot, self.half, self.me, self.n, self.dev = slot, half, me, n, dev
        self.send_sem, self.recv_sem, self.k = send_sem, recv_sem, n // 2

    def at(self, offset):
        return lax.rem(self.me + offset + self.n, self.n)

    def copies(self, s, shift):
        views = (self.slot, self.slot) if s < self.k - 1 else (lambda i: self.half(i, 0), lambda i: self.half(i, 1))
        out = []
        for way, sign in ((0, 1), (1, -1)):
            ref = views[way](self.at(-sign * (s + shift)))
            out.append(
                pltpu.make_async_remote_copy(
                    src_ref=ref,
                    dst_ref=ref,
                    send_sem=self.send_sem.at[way, s],
                    recv_sem=self.recv_sem.at[way, s],
                    device_id=self.dev(self.at(sign)),
                    device_id_type=MESH,
                )
            )
        return out

    def start(self, s):
        for copy in self.copies(s, 0):
            copy.start()

    def recv(self, s):
        for copy in self.copies(s, 1):
            copy.wait_recv()

    def finish(self):
        for s in range(self.k):
            for copy in self.copies(s, 0):
                copy.wait_send()


def quantize(value):
    largest = jnp.maximum(jnp.max(jnp.abs(value), axis=0, keepdims=True), 1e-30)
    whole = jnp.round(value * (32767.0 / largest)).astype(jnp.int32).astype(jnp.int16)
    return whole, largest * (1.0 / 32767.0)


def restore(whole, step):
    return whole.astype(jnp.int32).astype(F32) * step


class HalfRing:
    def __init__(self, half, me, n, right, left, send_sem, recv_sem):
        self.half, self.me, self.n, self.to = half, me, n, (right, left)
        self.send_sem, self.recv_sem = send_sem, recv_sem
        k = n // 2
        self.order = [(d, h) for d in range(k - 1) for h in (0, 1)] + [(k - 1, 0)]

    def copy(self, way, i, farther):
        d, h = self.order[i]
        d += farther
        ref = self.half(lax.rem(self.me + (d if way else self.n - d), self.n), 1 - h if way else h)
        return pltpu.make_async_remote_copy(
            src_ref=ref,
            dst_ref=ref,
            send_sem=self.send_sem.at[way, i],
            recv_sem=self.recv_sem.at[way, i],
            device_id=self.to[way],
            device_id_type=MESH,
        )

    def start(self, i):
        for way in range(2):
            self.copy(way, i, 0).start()

    def pass_on(self, i):
        for way in range(2):
            self.copy(way, i, 1).wait_recv()
            if i + 2 < len(self.order):
                self.copy(way, i + 2, 0).start()

    def finish(self):
        for i in range(len(self.order)):
            for way in range(2):
                self.copy(way, i, 0).wait_send()


class RingSum:
    def __init__(self, view, bufs, n, right, left, send_sem, recv_sem):
        self.view, self.n, self.to = view, n, (right, left)
        self.out, self.out_step, self.slots, self.steps = bufs
        self.send_sem, self.recv_sem = send_sem, recv_sem
        k = n // 2
        self.order = [(k, 0)] + [(j, h) for j in range(k - 1, 0, -1) for h in (1, 0)]
        self.rows, self.lanes = self.out.shape[2:]
        self.tall = self.rows == 512

    def part(self, way, i, nearer):
        j, h = self.order[i]
        j -= nearer
        return self.view((self.n - j) % self.n, 1 - h) if way else self.view(j, h)

    def copies(self, way, i):
        return [
            pltpu.make_async_remote_copy(
                src_ref=src.at[way, i],
                dst_ref=dst.at[way, i],
                send_sem=self.send_sem.at[way, i, t],
                recv_sem=self.recv_sem.at[way, i, t],
                device_id=self.to[way],
                device_id_type=MESH,
            )
            for t, (src, dst) in enumerate(((self.out, self.slots), (self.out_step, self.steps)))
        ]

    def groups(self):
        return [(g, slice(g * 64, (g + 1) * 64)) for g in range(8)] if self.tall else [(0, slice(0, self.rows))]

    def start(self, way, i):
        part = self.part(way, i, 0)
        steps = []
        for _, rows in self.groups():
            value = part[rows, :] if self.tall else part[...].reshape(self.rows, self.lanes)
            self.out[way, i, rows, :], step = quantize(value)
            steps.append(step)
        self.out_step[way, i] = jnp.concatenate(steps, 0) if self.tall else steps[0]
        for copy in self.copies(way, i):
            copy.start()

    def send(self, i):
        for way in range(2):
            self.start(way, i)

    def absorb(self, i):
        for way in range(2):
            for copy in self.copies(way, i):
                copy.wait_recv()
            part = self.part(way, i, 1)
            for g, rows in self.groups():
                value = restore(self.slots[way, i, rows, :], self.steps[way, i, g : g + 1, :])
                if self.tall:
                    part[rows, :] += value
                else:
                    part[...] += value.reshape(part.shape)
            if i + 2 < len(self.order):
                self.start(way, i + 2)

    def finish(self):
        for i in range(len(self.order)):
            for way in range(2):
                for copy in self.copies(way, i):
                    copy.wait_send()


def kernel(
    sizes,
    w_ref,
    x_ref,
    book_ref,
    codes_ref,
    pos_ref,
    wt_ref,
    wg_ref,
    cg_ref,
    g_all,
    w_full,
    xt,
    books,
    codes_t,
    pt,
    pas,
    qs,
    q_cat,
    exps,
    gs_cat,
    gn,
    gpt,
    normed_t,
    tots,
    ge_t,
    cg,
    cg_x,
    wz,
    wy,
    wzy_out,
    wzy_out_step,
    wzy_in,
    wzy_in_step,
    wyz_out,
    wyz_out_step,
    wyz_in,
    wyz_in_step,
    total,
    final,
    gn_out,
    gn_out_step,
    gn_in,
    gn_in_step,
    cg_out,
    cg_out_step,
    cg_in,
    cg_in_step,
    wz_out,
    wz_out_step,
    wz_got,
    wz_got_step,
    wy_out,
    wy_out_step,
    wy_got,
    wy_got_step,
    a1_s,
    a1_r,
    a2_s,
    a2_r,
    y_s,
    y_r,
    core_s,
    core_r,
    book_s,
    book_r,
    q_s,
    q_r,
    tot_s,
    tot_r,
    gn_s,
    gn_r,
    cx_s,
    cx_r,
    cz_s,
    cz_r,
    wc_s,
    wc_r,
    wz_s,
    wz_r,
    wy_s,
    wy_r,
    wzy_s,
    wzy_r,
    wyz_s,
    wyz_r,
    fin_s,
    fin_r,
):
    xh_n, y_n, c_n, z_n, x_n = sizes
    dom, z, x = lax.axis_index("dom"), lax.axis_index("shard"), lax.axis_index("dp")
    xh, y, c = dom // (y_n * c_n), lax.rem(dom // c_n, y_n), lax.rem(dom, c_n)

    def dom_of(xh_, y_, c_):
        return (xh_ * y_n + y_) * c_n + c_

    def dev(dom_=None, z_=None, x_=None):
        return {
            "dom": dom if dom_ is None else dom_,
            "shard": z if z_ is None else z_,
            "dp": x if x_ is None else x_,
        }

    def turn(i, d, n):
        return lax.rem(i + d + n, n)

    pending = []
    peers = [dev(z_=turn(z, dz, z_n)) for dz in range(1, z_n)] + [dev(x_=turn(x, 1, x_n))]
    peers += [dev(dom_of(turn(xh, 1, xh_n), y, c)), dev(dom_of(turn(xh, 1, xh_n), y, c), x_=turn(x, 1, x_n))]
    peers += [dev(dom_of(xh, turn(y, dy, y_n), c)) for dy in range(1, y_n)]
    peers += [dev(dom_of(xh, y, turn(c, 1, c_n)))]
    barrier = pltpu.get_barrier_semaphore()
    for peer in peers:
        pl.semaphore_signal(barrier, inc=1, device_id=peer, device_id_type=MESH)

    mine = x * z_n + z
    g_all[dom, mine] = w_ref[...]
    books[z] = book_ref[...].astype(BF16)
    pl.semaphore_wait(barrier, len(peers))

    def a1(d, back):
        z_ = turn(z, -d if back else d, z_n)
        ref = g_all.at[dom, x * z_n + z_ if back else mine]
        return pltpu.make_async_remote_copy(
            src_ref=ref,
            dst_ref=ref,
            send_sem=a1_s.at[d - 1],
            recv_sem=a1_r.at[d - 1],
            device_id=dev(z_=z_),
            device_id_type=MESH,
        )

    for d in range(1, z_n):
        a1(d, False).start()
        pending.append(a1(d, False).wait_send)
    book_ring = Ring(
        lambda i: books.at[i],
        lambda i, h: books.at[i, pl.ds(h * (books.shape[1] // 2), books.shape[1] // 2)],
        z,
        z_n,
        lambda i: dev(z_=i),
        book_s,
        book_r,
    )
    book_ring.start(0)
    pending.append(book_ring.finish)

    n_sub, n_pass = codes_t.shape
    for i in range(n_pass // 128):
        codes_t[:, i * 128 : (i + 1) * 128] = codes_ref[i * 128 : (i + 1) * 128, :].T
    for i in range(x_ref.shape[1] // 128):
        turned = x_ref[:, i * 128 : (i + 1) * 128].astype(F32).T.astype(BF16)
        for h in range(2):
            xt[h, i * 64 : (i + 1) * 64, :] = turned[h * 64 : (h + 1) * 64]

    xh2, x2 = turn(xh, 1, xh_n), turn(x, 1, x_n)

    def a2(k, back):
        dom_, x_ = dom_of(xh2 if k // 2 else xh, y, c), x2 if k % 2 else x
        ref = g_all.at[dom_ if back else dom, pl.ds((x_ if back else x) * z_n, z_n)]
        return pltpu.make_async_remote_copy(
            src_ref=ref,
            dst_ref=ref,
            send_sem=a2_s.at[k - 1],
            recv_sem=a2_r.at[k - 1],
            device_id=dev(dom_, x_=x_),
            device_id_type=MESH,
        )

    for d in range(1, z_n):
        a1(d, True).wait_recv()
    for k in range(1, 4):
        a2(k, False).start()
        pending.append(a2(k, False).wait_send)

    def y_ring(j, xh_):
        half = g_all.shape[1] // 2
        return Ring(
            lambda i: g_all.at[dom_of(xh_, i, c)],
            lambda i, h: g_all.at[dom_of(xh_, i, c), pl.ds(h * half, half)],
            y,
            y_n,
            lambda i: dev(dom_of(xh, i, c)),
            y_s.at[j],
            y_r.at[j],
        )

    def core(j, dy, back):
        ref = g_all.at[dom_of(xh2 if j else xh, turn(y, dy, y_n), turn(c, 1, c_n) if back else c)]
        return pltpu.make_async_remote_copy(
            src_ref=ref,
            dst_ref=ref,
            send_sem=core_s.at[j, dy],
            recv_sem=core_r.at[j, dy],
            device_id=dev(dom_of(xh, y, turn(c, 1, c_n))),
            device_id_type=MESH,
        )

    blk, col_blocks = w_ref.shape[0], x_ref.shape[1] // 128
    r_rows = blk // col_blocks
    per = 16 // r_rows
    rows = blk * per
    o = lax.broadcasted_iota(jnp.int32, (rows, rows), 0)
    j_ = lax.broadcasted_iota(jnp.int32, (rows, rows), 1)
    perm = (
        (j_ == (lax.rem(o, 16) // r_rows) * blk + (o // 16) * r_rows + lax.rem(o, r_rows)).astype(F32).astype(BF16)
    )

    def assemble(dom_):
        for t in range(g_all.shape[1] // per):
            blocks = [g_all[dom_, (b % x_n) * z_n + b // x_n] for b in range(t * per, (t + 1) * per)]
            part = jnp.dot(perm, jnp.concatenate(blocks, 0), preferred_element_type=F32).astype(BF16)
            row = pl.multiple_of((dom_ * (g_all.shape[1] // per) + t) * 16, 16)
            for cb in range(col_blocks):
                w_full[pl.ds(row, 16), cb * 128 : (cb + 1) * 128] = part[cb * 16 : (cb + 1) * 16]

    def rebuild(zb):
        groups = books.shape[1] // 64

        def per_group(gi, carry):
            r = pl.multiple_of(gi * 64, 64)
            table = books[zb, pl.ds(r, 64), :].astype(F32)
            out_row = pl.multiple_of(zb * books.shape[1] + r, 64)
            code_row = pl.multiple_of((zb * groups + gi) * 8, 8)

            def per_block(i, inner):
                for u in range(2):
                    p0 = pl.multiple_of(i * 256 + u * 128, 128)
                    cc = codes_t[pl.ds(code_row, 8), pl.ds(p0, 128)]
                    for jj in range(4):
                        parts = []
                        for j in (2 * jj, 2 * jj + 1):
                            idx = jnp.broadcast_to(cc[j : j + 1, :], (8, 128))
                            low = idx & 127
                            lo = jnp.take_along_axis(
                                table[j * 8 : j * 8 + 8, :128], low, axis=1, mode="promise_in_bounds"
                            )
                            hi = jnp.take_along_axis(
                                table[j * 8 : j * 8 + 8, 128:], low, axis=1, mode="promise_in_bounds"
                            )
                            parts.append(jnp.where(idx >= 128, hi, lo))
                        pt[pl.ds(pl.multiple_of(out_row + jj * 16, 16), 16), pl.ds(p0, 128)] = jnp.concatenate(
                            parts, 0
                        ).astype(BF16)
                return inner

            return lax.fori_loop(0, n_pass // 256, per_block, carry)

        lax.fori_loop(0, groups, per_group, 0)

    ring0, ring1 = y_ring(0, xh), y_ring(1, xh2)
    pending += [ring0.finish, ring1.finish]
    pending += [core(j, dy, False).wait_send for j in range(2) for dy in range(y_n)]
    a2(1, True).wait_recv()
    ring0.start(0)
    core(0, 0, False).start()
    a2(2, True).wait_recv()
    a2(3, True).wait_recv()
    ring1.start(0)
    core(1, 0, False).start()
    rebuild(z)
    book_ring.recv(0)
    book_ring.start(1)
    rebuild(turn(z, 1, z_n))
    ring0.recv(0)
    ring0.start(1)
    core(0, 1, False).start()
    core(0, 3, False).start()
    rebuild(turn(z, -1, z_n))
    book_ring.recv(1)
    book_ring.start(2)
    ring1.recv(0)
    ring1.start(1)
    core(1, 1, False).start()
    core(1, 3, False).start()
    assemble(dom_of(xh, y, c))
    assemble(dom_of(xh2, y, c))
    ring0.recv(1)
    core(0, 2, False).start()
    book_ring.recv(2)
    book_ring.start(3)
    for dy in (1, 3):
        assemble(dom_of(xh, turn(y, dy, y_n), c))
        assemble(dom_of(xh2, turn(y, dy, y_n), c))
    ring1.recv(1)
    core(1, 2, False).start()
    for j in range(2):
        assemble(dom_of(xh2 if j else xh, turn(y, 2, y_n), c))
    for dy in (0, 1, 3, 2):
        for j in range(2):
            core(j, dy, True).wait_recv()
            assemble(dom_of(xh2 if j else xh, turn(y, dy, y_n), turn(c, 1, c_n)))

    d_model = x_ref.shape[1]
    squares = jnp.zeros((1, 128), F32)
    for i in range(d_model // 256):
        enc = jnp.dot(x_ref[...], w_full[:, i * 256 : (i + 1) * 256], preferred_element_type=F32)
        for h in range(2):
            enc_t = enc[:, h * 128 : (h + 1) * 128].T
            squares = squares + jnp.sum(enc_t * enc_t, axis=0, keepdims=True)
            normed_t[i * 256 + h * 128 : i * 256 + (h + 1) * 128, :] = enc_t
    inv_rms = lax.rsqrt(squares / d_model + EPS)
    for i in range(d_model // 128):
        value = normed_t[i * 128 : (i + 1) * 128, :] * inv_rms
        normed_t[i * 128 : (i + 1) * 128, :] = value
        qs[z, i * 128 : (i + 1) * 128, :] = value.astype(BF16)

    half_d = d_model // 2
    right, left = dev(z_=turn(z, 1, z_n)), dev(z_=turn(z, -1, z_n))
    q_ring = HalfRing(lambda i, h: qs.at[i, pl.ds(h * half_d, half_d)], z, z_n, right, left, q_s, q_r)
    q_ring.start(0)
    q_ring.start(1)
    pending.append(q_ring.finish)
    rebuild(turn(z, 2, z_n))
    rebuild(turn(z, -2, z_n))
    q_ring.pass_on(0)
    rebuild(turn(z, 3, z_n))
    rebuild(turn(z, -3, z_n))
    q_ring.pass_on(1)
    book_ring.recv(3)
    rebuild(turn(z, 4, z_n))
    q_ring.pass_on(2)

    def flip(i, carry):
        f0 = pl.multiple_of(i * 128, 128)
        for t in range(n_pass // 128):
            pas[t * 128 : (t + 1) * 128, pl.ds(f0, 128)] = (
                pt[pl.ds(f0, 128), t * 128 : (t + 1) * 128].astype(F32).T.astype(BF16)
            )
        return carry

    lax.fori_loop(0, d_model // 128, flip, 0)

    sub8 = lax.broadcasted_iota(jnp.int32, (8, 128), 0)

    def score(j, totals):
        b = turn(z, j, z_n)
        block = qs[b]
        q_cat[:, j * 128 : (j + 1) * 128] = block
        total = jnp.zeros((1, 128), F32)
        for t in range(n_pass // 256):
            s = jnp.dot(pas[t * 256 : (t + 1) * 256, :], block, preferred_element_type=F32)
            e = jnp.exp(s)
            exps[j, t * 256 : (t + 1) * 256, :] = e
            total = total + jnp.sum(e, axis=0, keepdims=True)
        return totals + jnp.where(sub8 == b, jnp.broadcast_to(total, (8, 128)), 0.0)

    totals = score(0, jnp.zeros((8, 128), F32))
    q_ring.pass_on(3)
    totals = score(1, totals)
    totals = score(7, totals)
    q_ring.pass_on(4)
    totals = score(2, totals)
    totals = score(6, totals)
    q_ring.pass_on(5)
    totals = score(3, totals)
    totals = score(5, totals)
    q_ring.pass_on(6)
    totals = score(4, totals)

    tots[z] = totals

    def tot(d, back):
        other = turn(z, -d if back else d, z_n)
        ref = tots.at[other if back else z]
        return pltpu.make_async_remote_copy(
            src_ref=ref,
            dst_ref=ref,
            send_sem=tot_s.at[d - 1],
            recv_sem=tot_r.at[d - 1],
            device_id=dev(z_=other),
            device_id_type=MESH,
        )

    for d in range(1, z_n):
        tot(d, False).start()
        pending.append(tot(d, False).wait_send)
    for d in range(1, z_n):
        tot(d, True).wait_recv()
    totals = tots[0]
    for i in range(1, z_n):
        totals = totals + tots[i]
    inverse = 1.0 / totals

    sub16 = lax.broadcasted_iota(jnp.int32, (16, 128), 0)
    first = z * n_pass
    weights_all, pos_all = wt_ref[...], pos_ref[...]

    def grads(j):
        b = turn(z, j, z_n)
        inv = jnp.sum(jnp.where(sub8 == b, inverse, 0.0), axis=0, keepdims=True)
        wt = jnp.sum(jnp.where(sub16 == b * x_n + x, weights_all, 0.0), axis=0, keepdims=True)
        pos = jnp.sum(jnp.where(sub16 == b * x_n + x, pos_all, 0), axis=0, keepdims=True) - first
        for t in range(n_pass // 256):
            e = exps[j, t * 256 : (t + 1) * 256, :]
            ids = lax.broadcasted_iota(jnp.int32, (256, 128), 0) + t * 256
            prob = e * inv
            gs_cat[t * 256 : (t + 1) * 256, j * 128 : (j + 1) * 128] = (
                wt * jnp.where(ids == pos, prob - 1.0, prob)
            ).astype(BF16)
        block = gs_cat[:, j * 128 : (j + 1) * 128]
        for t in range(d_model // 256):
            gn[j, t * 256 : (t + 1) * 256, :] = jnp.dot(
                pt[t * 256 : (t + 1) * 256, :], block, preferred_element_type=F32
            )

    gn_ring = RingSum(
        lambda j, h: gn.at[j, pl.ds(h * half_d, half_d)], (gn_out, gn_out_step, gn_in, gn_in_step), z_n, right, left, gn_s, gn_r
    )
    pending.append(gn_ring.finish)
    grads(4)
    gn_ring.send(0)
    grads(3)
    grads(5)
    gn_ring.send(1)
    gn_ring.absorb(0)
    grads(2)
    grads(6)
    gn_ring.absorb(1)
    grads(1)
    grads(7)
    grads(0)

    def passage_grads(i, carry):
        p0 = pl.multiple_of(i * 256, 256)
        gpt[:, pl.ds(p0, 256)] = lax.dot_general(
            q_cat[...], gs_cat[pl.ds(p0, 256), :], NT, preferred_element_type=F32
        )
        return carry

    lax.fori_loop(0, n_pass // 256, passage_grads, 0)

    gn_ring.absorb(2)

    levels = lax.broadcasted_iota(jnp.int32, (64, n_pass), 0).astype(BF16)

    def scatter(lo_m, hi_m):
        def per_subs(i, carry):
            for u in range(4):
                m = i * 4 + u
                r = pl.multiple_of(m * 8, 8)
                code = codes_t[pl.ds(m, 1), :]
                low = (code & 63).astype(BF16)
                high = jnp.broadcast_to(lax.shift_right_logical(code, 6).astype(BF16), (16, n_pass))
                g = gpt[pl.ds(r, 8), :]
                g_hi = g.astype(BF16).astype(F32)
                g16 = jnp.concatenate([g_hi, g - g_hi], 0).astype(BF16)
                left = jnp.concatenate([jnp.where(high == BF16(h), g16, BF16(0)) for h in range(4)], 0)
                onehot = jnp.where(levels == jnp.broadcast_to(low, (64, n_pass)), BF16(1), BF16(0))
                out = lax.dot_general(left, onehot, NT, preferred_element_type=F32)
                cg[pl.ds(r, 8), :] = jnp.concatenate(
                    [out[h * 16 : h * 16 + 8] + out[h * 16 + 8 : h * 16 + 16] for h in range(4)], 1
                )
            return carry

        lax.fori_loop(lo_m // 4, hi_m // 4, per_subs, 0)

    own_rows = cg.shape[0] // (z_n * x_n)

    def own_words(zb, dp):
        return pl.ds(pl.multiple_of((zb * x_n + dp) * own_rows, own_rows), own_rows)

    def to_pair(zb):
        return pltpu.make_async_remote_copy(
            src_ref=cg.at[own_words(zb, turn(x, 1, x_n))],
            dst_ref=cg_x.at[zb],
            send_sem=cx_s.at[zb],
            recv_sem=cx_r.at[zb],
            device_id=dev(x_=turn(x, 1, x_n)),
            device_id_type=MESH,
        )

    def scatter_block(zb):
        scatter(zb * n_sub // z_n, (zb + 1) * n_sub // z_n)
        to_pair(zb).start()
        pending.append(to_pair(zb).wait_send)

    for zb in range(4):
        scatter_block(zb)
        gn_ring.absorb(zb + 3)

    inner = jnp.zeros((1, 128), F32)
    for i in range(d_model // 256):
        part = slice(i * 256, (i + 1) * 256)
        inner = inner + jnp.sum(gn[0, part, :] * normed_t[part, :], axis=0, keepdims=True)
    inner = inner / d_model
    for i in range(d_model // 256):
        part = slice(i * 256, (i + 1) * 256)
        ge_t[part, :] = (inv_rms * (gn[0, part, :] - normed_t[part, :] * inner)).astype(BF16)

    def share(i, core_, right_half):
        out = lax.dot_general(
            xt[core_], ge_t[half_d:, :] if right_half else ge_t[:half_d, :], NT, preferred_element_type=F32
        )
        for xh_ in range(xh_n):
            for y_ in range(y_n):
                for z_ in range(z_n):
                    tile = out[((xh_ * y_n + y_) * z_n + z_) * 8 : ((xh_ * y_n + y_) * z_n + z_) * 8 + 8]
                    if right_half:
                        wz[i, z_, xh_, y_] = tile
                    else:
                        wy[i, y_, xh_, z_] = tile

    sibling = turn(c, 1, c_n)

    def to_core(i):
        buf = (wz, wy)[i]
        return pltpu.make_async_remote_copy(
            src_ref=buf.at[1],
            dst_ref=buf.at[2],
            send_sem=wc_s.at[i],
            recv_sem=wc_r.at[i],
            device_id=dev(dom_of(xh, y, sibling)),
            device_id_type=MESH,
        )

    share(1, sibling, True)
    to_core(0).start()
    share(1, sibling, False)
    to_core(1).start()
    share(0, c, True)
    share(0, c, False)
    pending += [to_core(0).wait_send, to_core(1).wait_send]

    wz_ring = RingSum(
        lambda j, h: wz.at[0, turn(z, j, z_n), h], (wz_out, wz_out_step, wz_got, wz_got_step), z_n, right, left, wz_s, wz_r
    )
    wy_ring = RingSum(
        lambda j, h: wy.at[0, turn(y, j, y_n), h],
        (wy_out, wy_out_step, wy_got, wy_got_step),
        y_n,
        dev(dom_of(xh, turn(y, 1, y_n), c)),
        dev(dom_of(xh, turn(y, -1, y_n), c)),
        wy_s,
        wy_r,
    )

    def cg_half(j, h):
        row = (turn(z, j, z_n) * x_n + x) * own_rows + h * (own_rows // 2)
        return cg.at[pl.ds(pl.multiple_of(row, own_rows // 2), own_rows // 2)]

    cg_ring = RingSum(cg_half, (cg_out, cg_out_step, cg_in, cg_in_step), z_n, right, left, cz_s, cz_r)
    pending += [wz_ring.finish, wy_ring.finish, cg_ring.finish]

    to_core(0).wait_recv()
    for i in range(z_n):
        wz[0, i] += wz[2, i]
    for i in range(2):
        wz_ring.send(i)
    to_core(1).wait_recv()
    for i in range(y_n):
        wy[0, i] += wy[2, i]
    for i in range(2):
        wy_ring.send(i)
    def direct(bufs, send_sem, recv_sem, d, target):
        out, out_step, got, got_step = bufs
        return [
            pltpu.make_async_remote_copy(
                src_ref=src.at[d - 1],
                dst_ref=dst.at[d - 1],
                send_sem=send_sem.at[d - 1, t],
                recv_sem=recv_sem.at[d - 1, t],
                device_id=target,
                device_id_type=MESH,
            )
            for t, (src, dst) in enumerate(((out, got), (out_step, got_step)))
        ]

    wzy_bufs = (wzy_out, wzy_out_step, wzy_in, wzy_in_step)
    wyz_bufs = (wyz_out, wyz_out_step, wyz_in, wyz_in_step)

    def wzy(d):
        return direct(wzy_bufs, wzy_s, wzy_r, d, dev(dom_of(xh, turn(y, d, y_n), c)))

    def wyz(d):
        return direct(wyz_bufs, wyz_s, wyz_r, d, dev(z_=turn(z, d, z_n)))

    def spread(view, bufs, copies, n):
        for d in range(1, n):
            bufs[0][d - 1], bufs[1][d - 1] = quantize(view(d).reshape(xh_n * 8, half_d))
            for copy in copies(d):
                copy.start()
                pending.append(copy.wait_send)

    def collect(view, bufs, copies, n):
        acc = view(0).reshape(xh_n * 8, half_d)
        for d in range(1, n):
            for copy in copies(d):
                copy.wait_recv()
            acc = acc + restore(bufs[2][d - 1], bufs[3][d - 1])
        return acc.reshape(xh_n, 8, half_d)

    def wz_part(d):
        return wz[0, z, :, turn(y, d, y_n)]

    def wy_part(d):
        return wy[0, y, :, turn(z, d, z_n)]

    for i in range(3):
        scatter_block(4 + i)
        wz_ring.absorb(i)
        wy_ring.absorb(i)
    spread(wy_part, wyz_bufs, wyz, z_n)
    scatter_block(7)
    wz_ring.absorb(3)
    for zb in range(z_n):
        to_pair(zb).wait_recv()
        cg[own_words(zb, x), :] += cg_x[zb]
    for i in range(2):
        cg_ring.send(i)
    for i in range(3):
        wz_ring.absorb(4 + i)
        cg_ring.absorb(i)
    spread(wz_part, wzy_bufs, wzy, y_n)
    cg_ring.absorb(3)
    total[:, :, :half_d] = collect(wy_part, wyz_bufs, wyz, z_n)
    total[:, :, half_d:] = collect(wz_part, wzy_bufs, wzy, y_n)

    def last(k):
        xh_, x_ = turn(xh, k // 2, xh_n), turn(x, k % 2, x_n)
        return pltpu.make_async_remote_copy(
            src_ref=total.at[xh_],
            dst_ref=final.at[k - 1],
            send_sem=fin_s.at[k - 1],
            recv_sem=fin_r.at[k - 1],
            device_id=dev(dom_of(xh_, y, c), x_=x_),
            device_id_type=MESH,
        )

    for k in range(1, 4):
        last(k).start()
        pending.append(last(k).wait_send)
    for i in range(4, 7):
        cg_ring.absorb(i)
    cg_ref[...] = cg[own_words(z, x), :]
    acc = total[xh]
    for k in range(1, 4):
        last(k).wait_recv()
        acc = acc + final[k - 1]
    wg_ref[...] = jnp.where(x == 0, acc[:4], acc[4:])

    for wait in pending:
        wait()


def per_device(sizes, queries_in, encoder_weight, codebook, codes, positive_ids, loss_weight):
    xh_n, y_n, c_n, z_n, x_n = sizes
    q_rows, d_model = queries_in.shape[1:]
    w_rows = encoder_weight.shape[0]
    subs, width, words = codebook.shape[1:]
    n_pass, n_sub = codes.shape[1:]
    blk = w_rows * d_model // 128
    group, doms, half = z_n * x_n, xh_n * y_n * c_n, d_model // 2
    w = encoder_weight.reshape(w_rows, d_model // 128, 128).transpose(1, 0, 2).reshape(blk, 128)

    def ring_bufs(n, rows, lanes):
        return 2 * [
            pltpu.VMEM((2, n - 1, rows, lanes), jnp.int16),
            pltpu.VMEM((2, n - 1, 8 if rows == 512 else 1, lanes), F32),
        ]

    def direct_bufs(n, rows, lanes):
        return 2 * [pltpu.VMEM((n - 1, rows, lanes), jnp.int16), pltpu.VMEM((n - 1, 1, lanes), F32)]

    vmem = pl.BlockSpec(memory_space=pltpu.VMEM)
    dma = pltpu.SemaphoreType.DMA
    wg, cg = pl.pallas_call(
        functools.partial(kernel, sizes),
        out_shape=(
            jax.ShapeDtypeStruct((w_rows, d_model), F32),
            jax.ShapeDtypeStruct((d_model // group, words), F32),
        ),
        in_specs=[vmem] * 6,
        out_specs=(vmem, vmem),
        scratch_shapes=[
            pltpu.VMEM((doms, group, blk, 128), BF16),
            pltpu.VMEM((d_model, d_model), BF16),
            pltpu.VMEM((2, d_model // 2, q_rows), BF16),
            pltpu.VMEM((z_n, subs * width, words), BF16),
            pltpu.VMEM((n_sub, n_pass), jnp.int32),
            pltpu.VMEM((d_model, n_pass), BF16),
            pltpu.VMEM((n_pass, d_model), BF16),
            pltpu.VMEM((z_n, d_model, q_rows), BF16),
            pltpu.VMEM((d_model, z_n * q_rows), BF16),
            pltpu.VMEM((z_n, n_pass, q_rows), F32),
            pltpu.VMEM((n_pass, z_n * q_rows), BF16),
            pltpu.VMEM((z_n, d_model, q_rows), F32),
            pltpu.VMEM((d_model, n_pass), F32),
            pltpu.VMEM((d_model, q_rows), F32),
            pltpu.VMEM((z_n, 8, 128), F32),
            pltpu.VMEM((d_model, q_rows), BF16),
            pltpu.VMEM((d_model, words), F32),
            pltpu.VMEM((z_n, d_model // group, words), F32),
            pltpu.VMEM((3, z_n, xh_n, y_n, 8, half), F32),
            pltpu.VMEM((3, y_n, xh_n, z_n, 8, half), F32),
            *direct_bufs(y_n, xh_n * 8, half),
            *direct_bufs(z_n, xh_n * 8, half),
            pltpu.VMEM((xh_n, 8, d_model), F32),
            pltpu.VMEM((3, 8, d_model), F32),
            *ring_bufs(z_n, half, q_rows),
            *ring_bufs(z_n, d_model // group // 2, words),
            *ring_bufs(z_n, y_n * 8, half),
            *ring_bufs(y_n, z_n * 8, half),
            dma((z_n - 1,)),
            dma((z_n - 1,)),
            dma((3,)),
            dma((3,)),
            dma((2, 2, y_n // 2)),
            dma((2, 2, y_n // 2)),
            dma((2, y_n)),
            dma((2, y_n)),
            dma((2, z_n // 2)),
            dma((2, z_n // 2)),
            dma((2, z_n - 1)),
            dma((2, z_n - 1)),
            dma((z_n - 1,)),
            dma((z_n - 1,)),
            dma((2, z_n - 1, 2)),
            dma((2, z_n - 1, 2)),
            dma((z_n,)),
            dma((z_n,)),
            dma((2, z_n - 1, 2)),
            dma((2, z_n - 1, 2)),
            dma((2,)),
            dma((2,)),
            dma((2, z_n - 1, 2)),
            dma((2, z_n - 1, 2)),
            dma((2, y_n - 1, 2)),
            dma((2, y_n - 1, 2)),
            dma((y_n - 1, 2)),
            dma((y_n - 1, 2)),
            dma((z_n - 1, 2)),
            dma((z_n - 1, 2)),
            dma((3,)),
            dma((3,)),
        ],
        compiler_params=pltpu.CompilerParams(
            collective_id=0, has_side_effects=True, vmem_limit_bytes=60 * 2**20
        ),
        name="encoder_codebook_grads",
    )(
        w,
        queries_in[0],
        codebook.reshape(subs * width, words),
        codes[0],
        positive_ids.reshape(group, q_rows),
        loss_weight.reshape(group, q_rows).astype(F32),
    )
    return wg, cg.reshape(1, n_sub // group, width, words)


def solution(mesh):
    doms = mesh.shape["dom"]
    sizes = (2, doms // 4, 2, mesh.shape["shard"], mesh.shape["dp"])
    return jax.shard_map(
        functools.partial(per_device, sizes),
        mesh=mesh,
        in_specs=(
            P("dom", ("shard", "dp"), None),
            P(("dom", "shard", "dp"), None),
            P("dom", "shard", None, None),
            P("dom", "shard", None),
            P("dom", None),
            P("dom", None),
        ),
        out_specs=(P(("dom", "shard", "dp"), None), P("dom", ("shard", "dp"), None, None)),
        check_vma=False,
    )
```

profile of v0, /device:TPU:2, one launch (start us, length us, event | category | flops | bytes accessed | tf_op | source)
XLA Modules:
  0.0 121.8 jit_solution(1750975524442199925)
XLA Ops:
  0.6 0.0 copy-start
  0.6 0.7 copy-done
  1.3 0.6 convert_element_type.7
  1.9 117.0 %encoder_codebook_grads.1 = (f32[4,1024]{1,0:T(4,128)}, f32[64,256]{1,0:T(8,128)}) custom-call(bf16[32,128]{1,0:T(8,128)(2,1)} %bitcast.16, bf16[128,1024]{1,0:T(8,128)(2,1)} %bitcast.12, f32[128,256]{1,0:T(8,128)} %bitcast.13, s32[1024,128]{1,0:T(8,128)} %bitcast.11, s32[16,128]{1,0:T(8,128)} %bitcast.17, f32[16,128]{1,0:T(8,128)} %bitcast.15), custom_call_target="tpu_custom_call" | custom-call | tf_op jit(solution)/shard_map/encoder_codebook_grads/pallas_call | solution.py:835
  119.0 1.3 %copy.11 = f32[4,1024]{1,0:T(4,128)} copy(f32[4,1024]{1,0:T(4,128)} %get-tuple-element.8) | data formatting | bytes 32768
  120.3 1.5 %copy.12 = f32[1,8,8,256]{3,2,1,0:T(8,128)} copy(f32[1,8,8,256]{3,2,1,0:T(8,128)} %bitcast.14) | data formatting | bytes 131072
Async XLA Ops:
  0.6 0.7 copy-start
where the time goes:
time: 122 us
  Pallas kernels  117 us (96%)
  local copies, waits for them, and re-layouts  3.49 us (3%)
    pallas_call x1, Pallas kernels, per_device(): pl.pallas_call(functools.partial(kernel, sizes), out_shape=(jax.ShapeDtyp...  117 us
    unnamed x4, local copies, waits for them, and re-layouts  3.49 us

commit v1 on v0

--- a/solution.py
+++ b/solution.py
@@ -781,29 +781,30 @@
         cg_ring.absorb(i)
     spread(wz_part, wzy_bufs, wzy, y_n)
     cg_ring.absorb(3)
-    total[:, :, :half_d] = collect(wy_part, wyz_bufs, wyz, z_n)
-    total[:, :, half_d:] = collect(wz_part, wzy_bufs, wzy, y_n)
-
-    def last(k):
+    def last(k, h):
         xh_, x_ = turn(xh, k // 2, xh_n), turn(x, k % 2, x_n)
+        columns = pl.ds(h * half_d, half_d)
         return pltpu.make_async_remote_copy(
-            src_ref=total.at[xh_],
-            dst_ref=final.at[k - 1],
-            send_sem=fin_s.at[k - 1],
-            recv_sem=fin_r.at[k - 1],
+            src_ref=total.at[xh_, :, columns],
+            dst_ref=final.at[k - 1, :, columns],
+            send_sem=fin_s.at[k - 1, h],
+            recv_sem=fin_r.at[k - 1, h],
             device_id=dev(dom_of(xh_, y, c), x_=x_),
             device_id_type=MESH,
         )
 
-    for k in range(1, 4):
-        last(k).start()
-        pending.append(last(k).wait_send)
+    for h, args in ((0, (wy_part, wyz_bufs, wyz, z_n)), (1, (wz_part, wzy_bufs, wzy, y_n))):
+        total[:, :, h * half_d : (h + 1) * half_d] = collect(*args)
+        for k in range(1, 4):
+            last(k, h).start()
+            pending.append(last(k, h).wait_send)
     for i in range(4, 7):
         cg_ring.absorb(i)
     cg_ref[...] = cg[own_words(z, x), :]
     acc = total[xh]
     for k in range(1, 4):
-        last(k).wait_recv()
+        for h in range(2):
+            last(k, h).wait_recv()
         acc = acc + final[k - 1]
     wg_ref[...] = jnp.where(x == 0, acc[:4], acc[4:])
 
@@ -899,8 +900,8 @@
             dma((y_n - 1, 2)),
             dma((z_n - 1, 2)),
             dma((z_n - 1, 2)),
-            dma((3,)),
-            dma((3,)),
+            dma((3, 2)),
+            dma((3, 2)),
         ],
         compiler_params=pltpu.CompilerParams(
             collective_id=0, has_side_effects=True, vmem_limit_bytes=60 * 2**20

time: 122 us -> 122 us (level)
  no operation moved by 1% of the time
where the time goes in v1:
time: 122 us
  Pallas kernels  117 us (96%)
  local copies, waits for them, and re-layouts  3.49 us (3%)
    pallas_call x1, Pallas kernels, per_device(): pl.pallas_call(functools.partial(kernel, sizes), out_shape=(jax.ShapeDtyp...  117 us
    unnamed x4, local copies, waits for them, and re-layouts  3.49 us

profile of v1, /device:TPU:2, one launch (start us, length us, event | category | flops | bytes accessed | tf_op | source)
XLA Modules:
  0.0 121.8 jit_solution(9991200917969335164)
XLA Ops:
  0.6 0.0 copy-start
  0.6 0.7 copy-done
  1.3 0.6 convert_element_type.7
  1.9 117.1 %encoder_codebook_grads.1 = (f32[4,1024]{1,0:T(4,128)}, f32[64,256]{1,0:T(8,128)}) custom-call(bf16[32,128]{1,0:T(8,128)(2,1)} %bitcast.16, bf16[128,1024]{1,0:T(8,128)(2,1)} %bitcast.12, f32[128,256]{1,0:T(8,128)} %bitcast.13, s32[1024,128]{1,0:T(8,128)} %bitcast.11, s32[16,128]{1,0:T(8,128)} %bitcast.17, f32[16,128]{1,0:T(8,128)} %bitcast.15), custom_call_target="tpu_custom_call" | custom-call | tf_op jit(solution)/shard_map/encoder_codebook_grads/pallas_call | solution.py:836
  119.0 1.3 %copy.11 = f32[4,1024]{1,0:T(4,128)} copy(f32[4,1024]{1,0:T(4,128)} %get-tuple-element.8) | data formatting | bytes 32768
  120.4 1.5 %copy.12 = f32[1,8,8,256]{3,2,1,0:T(8,128)} copy(f32[1,8,8,256]{3,2,1,0:T(8,128)} %bitcast.14) | data formatting | bytes 131072
Async XLA Ops:
  0.6 0.7 copy-start
